TPU v7x, 32 devices: a whole 2x2x4 slice. The times are simulated.
32 devices in a mesh: layer: 16 (over z, x, core), row: 2 (over y).
Axes of the slice: x: 2, y: 2, z: 4, core: 2. Of those that a mesh axis runs over, the one named last changes fastest.
Arguments:
- coupling: bfloat16 [16, 1024, 1024], P('layer', 'row'), may hold values from -1 to 1, as said below
- band_off: int32 [16], P('layer'), may hold values from 0 to 32
- band_width: int32 [16], P('layer'), may hold values from 1 to 3
- incident: float32 [32, 1024], P(None, 'row'), may hold values from -6 to 6
- cotangent: float32 [32, 1024], P(None, 'row'), may hold values from -6 to 6
Outputs:
- transmitted: float32 [16, 32, 1024], P('layer', None, 'row')
- adjoint: float32 [16, 32, 1024], P('layer', None, 'row')
Inputs may be any that keep to these rules, and one draw needn't show every extreme that they name: coupling is antisymmetric in its last two dimensions.
All inputs are finite; a program needn't handle non-finite values.
Results may differ from a plain program's by a relative error of at most 0.012.
The roundings to bfloat16 on the way count: a program that leaves them out, or rounds other values in their place, can miss the bound.
Values may be sent and summed in bfloat16 or wider, within the bound.
No kernel may reach another device: no remote copies, remote signals or barrier semaphores. Data moves between devices by JAX's collectives and lax.ppermute only.
A program may use at most 64 MiB of HBM per device.

v0:
```python
import functools

import jax
import jax.numpy as jnp
from jax import lax
from jax.experimental import pallas as pl
from jax.experimental.pallas import tpu as pltpu
from jax.sharding import PartitionSpec as P

BLOCK = 16
GROUP = 8
LANES = 128
BLOCKS_PER_LANES = LANES // BLOCK
PACKED = LANES - BLOCK
DEGREE = 4
SMALL_GRANT = 4 * 1024 * 1024
FIELD_PARTS = GROUP // 2


def field_rows(fields, panel):
    return -(-fields // FIELD_PARTS * (panel // LANES) // BLOCK) * BLOCK


def fold_kernel(
    off_ref, width_ref, coupling_ref, field_ref, folded_ref
):
    rows, orders = coupling_ref.shape[1:]
    slot = lax.axis_index("layer") % GROUP
    fields, panel = field_ref.shape
    part = fields // FIELD_PARTS
    mine = field_ref[pl.ds(pl.multiple_of(slot // 2 * part, part), part), :]
    sent = [mine[:, u : u + LANES] for u in range(0, panel, LANES)]
    spare = field_rows(fields, panel) - part * len(sent)
    if spare:
        sent.append(jnp.zeros((spare, LANES), jnp.float32))
    sent = jnp.concatenate(sent, axis=0).astype(jnp.bfloat16)
    folded_ref[panel // LANES * PACKED :, :] = sent
    first = off_ref[0] - width_ref[0]
    last = off_ref[0] + width_ref[0]
    first_block = lax.axis_index("row") * (rows // BLOCK)
    lane = lax.broadcasted_iota(jnp.int32, (BLOCK, LANES), 1)
    sub = lax.broadcasted_iota(jnp.int32, (BLOCK, LANES), 0)
    top = orders // LANES - 1
    for local in range(rows // BLOCK):
        if local % BLOCKS_PER_LANES == 0:
            runs = []
        block = first_block + local
        start = (block + first) * BLOCK
        tile = start >> 7
        shift = start & (LANES - 1)
        here = slice(local * BLOCK, (local + 1) * BLOCK)

        def part(index):
            column = pl.multiple_of(jnp.clip(index, 0, top) * LANES, LANES)
            return coupling_ref[0, here, pl.ds(column, LANES)].astype(jnp.float32)

        near = lane >= shift
        column = jnp.where(near, lane, lane + LANES) + tile * LANES
        limit = jnp.minimum((block + last + 1) * BLOCK, orders)
        keep = (column > block * BLOCK + sub) & (column < limit)
        folded = jnp.where(keep, jnp.where(near, part(tile), part(tile + 1)), 0.0)
        is_last = block * BLOCK + sub == orders - 1
        folded = jnp.where(is_last, first.astype(jnp.float32), folded)
        runs.append(pltpu.roll(folded, (-first * BLOCK) & (LANES - 1), 1))
        if len(runs) == BLOCKS_PER_LANES:
            base = local * BLOCK // LANES * PACKED
            for b, run in enumerate(runs[:-1]):
                hole = lane // BLOCK == (b - 1) % BLOCKS_PER_LANES
                folded_ref[base + b * BLOCK : base + (b + 1) * BLOCK, :] = jnp.where(
                    hole, runs[-1], run
                ).astype(jnp.bfloat16)


def fold(coupling, band_off, band_width, field):
    rows, orders = coupling.shape[1:]
    sent = rows // LANES * PACKED + field_rows(*field.shape)
    smem = pl.BlockSpec(memory_space=pltpu.SMEM)
    vmem = pl.BlockSpec(memory_space=pltpu.VMEM)
    return pl.pallas_call(
        fold_kernel,
        out_shape=jax.ShapeDtypeStruct((sent, LANES), jnp.bfloat16),
        in_specs=[smem, smem, vmem, vmem],
        out_specs=vmem,
        compiler_params=pltpu.CompilerParams(vmem_limit_bytes=SMALL_GRANT),
        name="fold",
    )(band_off, band_width, coupling, field)


def batch_kernel(*refs):
    for index, piece in enumerate(refs[:-1]):
        refs[-1][index] = piece[...]


def batch(pieces):
    vmem = pl.BlockSpec(memory_space=pltpu.VMEM)
    return pl.pallas_call(
        batch_kernel,
        out_shape=jax.ShapeDtypeStruct((len(pieces), *pieces[0].shape), pieces[0].dtype),
        in_specs=[vmem] * len(pieces),
        out_specs=vmem,
        compiler_params=pltpu.CompilerParams(vmem_limit_bytes=SMALL_GRANT),
        name="batch",
    )(*pieces)


def place(pieces, distances, folds):
    slot = lax.axis_index("layer") % GROUP
    row = lax.axis_index("row")
    rows = folds.shape[1] // lax.axis_size("row")
    for (ref, index), (layer_mask, row_mask) in zip(pieces, distances):
        here = pl.ds(pl.multiple_of((row ^ row_mask) * rows, BLOCK), rows)
        folds[slot ^ layer_mask, here, :] = ref[index, :rows, :]


def place_field(own, pieces, distances, field):
    slot = lax.axis_index("layer") % GROUP
    row = lax.axis_index("row")
    fields, panel = own.shape
    part, tiles = fields // FIELD_PARTS, panel // LANES
    for u in range(tiles):
        field[row * tiles + u] = own[:, u * LANES : (u + 1) * LANES]
    for (ref, index), (layer_mask, row_mask) in zip(pieces, distances):
        if row_mask and not layer_mask & 1:
            here = pl.ds(pl.multiple_of((slot ^ layer_mask) // 2 * part, part), part)
            sent = ref[index, tiles * PACKED :, :].astype(jnp.float32)
            for u in range(tiles):
                field[(row ^ row_mask) * tiles + u, here, :] = sent[u * part : (u + 1) * part]


def fill_masks(masks):
    row = lax.broadcasted_iota(jnp.int32, (LANES, LANES), 0)
    lane = lax.broadcasted_iota(jnp.int32, (LANES, LANES), 1)
    masks[0] = (lane >= row // BLOCK * BLOCK).astype(jnp.float32).astype(jnp.bfloat16)
    masks[1] = (row >= lane // BLOCK * BLOCK).astype(jnp.float32).astype(jnp.bfloat16)
    masks[2] = (row < LANES - 1).astype(jnp.float32).astype(jnp.bfloat16)
    own = lane // BLOCK != (row // BLOCK + BLOCKS_PER_LANES - 1) % BLOCKS_PER_LANES
    masks[3] = own.astype(jnp.float32).astype(jnp.bfloat16)


def expand(folds, slot, masks, upper, lower):
    tiles = upper.shape[0]
    lane = lax.broadcasted_iota(jnp.int32, (1, LANES), 1)
    eighth = folds[slot, (tiles - 1) * PACKED : (tiles - 1) * PACKED + BLOCK, :]
    last_row = eighth.astype(jnp.float32)[BLOCK - 1 :, :]
    last_row = jnp.where(lane >= PACKED, last_row, -float(LANES))
    first = jnp.max(last_row).astype(jnp.int32)
    for t in range(tiles):
        packed = folds[slot, t * PACKED : (t + 1) * PACKED, :]
        own = packed * masks[3, :PACKED, :]
        rest = packed - own
        eighth = [rest[b : b + BLOCK] for b in range(0, PACKED, BLOCK)]
        while len(eighth) > 1:
            eighth = [sum(eighth[i : i + 2][1:], eighth[i]) for i in range(0, len(eighth), 2)]
        run = jnp.concatenate([own, eighth[0]], axis=0)
        if t == tiles - 1:
            run = run * masks[2]
        near = run * masks[0]
        upper[t, :, :LANES] = near
        upper[t, :, LANES:] = run - near
        turned = run.T
        near = turned * masks[1]
        lower[t, :, :LANES] = near
        lower[(t + 1) % tiles, :, LANES:] = turned - near
    return first


def banded_product(v, upper, lower, start, xs, zs):
    tiles = len(v)
    whole = start >> 3
    fine = (start & (BLOCKS_PER_LANES - 1)) * BLOCK
    lane = lax.broadcasted_iota(jnp.int32, v[0].shape, 1)
    turned = [pltpu.roll(part, (LANES - fine) & (LANES - 1), 1) for part in v]
    for u in range(tiles):
        moved = jnp.where(lane < LANES - fine, turned[u], turned[(u + 1) % tiles])
        xs[u] = moved.astype(jnp.bfloat16)
    first = [
        jnp.dot(v[t].astype(jnp.bfloat16), upper[t], preferred_element_type=jnp.float32)
        for t in range(tiles)
    ]
    sums = [first[t][:, :LANES] + first[t - 1][:, LANES:] for t in range(tiles)]
    turned = [pltpu.roll(part, fine, 1) for part in sums]
    for u in range(tiles):
        zs[u] = jnp.where(lane >= fine, turned[u], turned[u - 1])
    second = [
        jnp.dot(
            xs[(whole + u) & (tiles - 1)], lower[u], preferred_element_type=jnp.float32
        )
        for u in range(tiles)
    ]
    return [
        zs[(u - whole) & (tiles - 1)]
        - (second[u][:, :LANES] + second[(u + 1) % tiles][:, LANES:])
        for u in range(tiles)
    ]


def run_layer(x, sign, upper, lower, start, xs, zs):
    v = x
    for divisor in range(DEGREE, 0, -1):
        scale = sign * (1.0 / divisor)
        product = banded_product(v, upper, lower, start, xs, zs)
        v = [part + scale * term for part, term in zip(x, product)]
    return v


def cascade_first_kernel(distances, *refs):
    pieces = []
    for count in distances[0]:
        pieces += [(refs[0], index) for index in range(count)]
        refs = refs[1:]
    own, kept, upper, lower, starts, send, folds, masks, xs, zs = refs
    place(pieces, distances[1], folds)
    fill_masks(masks)
    place_field(own, pieces, distances[1], zs)
    x = [zs[u] for u in range(zs.shape[0])]
    forward = lax.axis_index("layer") // GROUP == 0
    sign = jnp.where(forward, -1.0, 1.0)

    def prepare(k):
        slot = jnp.where(forward, k, GROUP - 1 - k)
        start = expand(folds, slot, masks, upper.at[k], lower.at[k])
        starts[k : k + 1, :] = jnp.full((1, LANES), start, jnp.int32)
        return start

    start = prepare(0)
    for k in range(GROUP):
        following = prepare(k + 1) if k + 1 < GROUP else None
        x = run_layer(x, sign, upper.at[k], lower.at[k], start, xs, zs)
        start = following
    finish(x, kept, send)


def cascade_next_kernel(step, groups, *refs):
    upper, lower, starts, field, kept_forward, kept_adjoint = refs[:6]
    new_forward, new_adjoint, *send, xs, zs = refs[6:]
    group = lax.axis_index("layer") // GROUP
    forward = group == step
    backward = group == groups - 1 - step
    sign = jnp.where(forward, -1.0, 1.0)
    same_order = forward == (group == 0)
    x = field[...].astype(jnp.float32)
    x = [x[:, u : u + LANES] for u in range(0, x.shape[1], LANES)]

    def layer(k, x):
        at = jnp.where(same_order, k, GROUP - 1 - k)
        start = jnp.max(starts[pl.ds(at, 1), :])
        return run_layer(x, sign, upper.at[at], lower.at[at], start, xs, zs)

    x = lax.fori_loop(0, GROUP, layer, x)
    finish(x, new_forward, *send)
    mine = new_forward[0]
    new_forward[0] = jnp.where(forward, mine, kept_forward[0])
    new_adjoint[0] = jnp.where(backward, mine, kept_adjoint[0])


def finish(x, mine_ref, send=None):
    row = lax.axis_index("row")
    panel = mine_ref.shape[-1]
    if send is not None:
        for u, part in enumerate(x):
            send[:, u * LANES : (u + 1) * LANES] = part.astype(jnp.bfloat16)
    tiles = panel // LANES
    for u in range(tiles):
        mine = x[u]
        for index in range(1, len(x) // tiles):
            mine = jnp.where(row == index, x[index * tiles + u], mine)
        mine_ref[0, :, u * LANES : (u + 1) * LANES] = mine


def run_first(batches, distances, field, orders):
    count, panel = field.shape
    tiles = orders // LANES
    vmem = pl.BlockSpec(memory_space=pltpu.VMEM)
    window = jax.ShapeDtypeStruct((GROUP, tiles, LANES, 2 * LANES), jnp.bfloat16)
    return pl.pallas_call(
        functools.partial(cascade_first_kernel, distances),
        out_shape=[
            jax.ShapeDtypeStruct((1, count, panel), jnp.float32),
            window,
            window,
            jax.ShapeDtypeStruct((GROUP, LANES), jnp.int32),
            jax.ShapeDtypeStruct((count, orders), jnp.bfloat16),
        ],
        in_specs=[vmem] * (len(batches) + 1),
        out_specs=[vmem] * 5,
        scratch_shapes=[
            pltpu.VMEM((GROUP, tiles * PACKED, LANES), jnp.bfloat16),
            pltpu.VMEM((4, LANES, LANES), jnp.bfloat16),
            pltpu.VMEM((tiles, count, LANES), jnp.bfloat16),
            pltpu.VMEM((tiles, count, LANES), jnp.float32),
        ],
        compiler_params=pltpu.CompilerParams(vmem_limit_bytes=24 * 1024 * 1024),
        name="cascade_first",
    )(*batches, field)


def run_next(step, groups, upper, lower, starts, field, kept):
    count, orders = field.shape
    tiles = orders // LANES
    vmem = pl.BlockSpec(memory_space=pltpu.VMEM)
    out_shape = [jax.ShapeDtypeStruct(kept[0].shape, jnp.float32)] * 2
    if step < groups - 1:
        out_shape.append(jax.ShapeDtypeStruct(field.shape, jnp.bfloat16))
    return pl.pallas_call(
        functools.partial(cascade_next_kernel, step, groups),
        out_shape=out_shape,
        in_specs=[vmem] * 6,
        out_specs=[vmem] * len(out_shape),
        scratch_shapes=[
            pltpu.VMEM((tiles, count, LANES), jnp.bfloat16),
            pltpu.VMEM((tiles, count, LANES), jnp.float32),
        ],
        compiler_params=pltpu.CompilerParams(vmem_limit_bytes=24 * 1024 * 1024),
        name=f"cascade_{step}",
    )(upper, lower, starts, field, *kept)


def gather_batches(own, across, rows):
    bits = [(0, 1 << b) for b in range(rows.bit_length() - 1)]
    bits += [(1 << b, 0) for b in range(1, GROUP.bit_length() - 1)]
    count = len(bits)

    def members(subset):
        return [b for b in range(count) if subset >> b & 1]

    def distance(subset):
        return tuple(sum(bits[b][axis] for b in members(subset)) for axis in (0, 1))

    subsets = sorted(range(1 << count), key=lambda m: (m.bit_count(), m))
    pieces = {0: own}
    for subset in subsets[1 : count + 1] + subsets[-1:]:
        pieces[subset] = across(own, *distance(subset))
    for subset in subsets[count + 1 : -1]:
        which = members(subset)
        link = next((b for b in which if (b + 1) % count in which), which[0])
        pieces[subset] = across(pieces[subset ^ 1 << link], *distance(1 << link))
    batches, counts, distances = [], [], []
    for part in (subsets[: count + 1], subsets[count + 1 :]):
        mine = batch([pieces[subset] for subset in part])
        batches += [mine, across(mine, 1, 0)]
        counts += [len(part), len(part)]
        distances += [distance(subset) for subset in part]
        distances += [(a ^ 1, b) for a, b in distances[-len(part) :]]
    return batches, (tuple(counts), tuple(distances))


def on_device(coupling, band_off, band_width, incident, cotangent):
    panel, orders = coupling.shape[1:]
    layers = lax.axis_size("layer")
    rows = lax.axis_size("row")
    groups = layers // GROUP

    def across(array, layer_mask, row_mask):
        pairs = [
            (l * rows + r, (l ^ layer_mask) * rows + (r ^ row_mask))
            for l in range(layers)
            for r in range(rows)
        ]
        return lax.ppermute(array, ("layer", "row"), pairs)

    field = jnp.where(lax.axis_index("layer") // GROUP == 0, incident, cotangent)
    folded = fold(coupling, band_off, band_width, field)
    batches, distances = gather_batches(folded, across, rows)

    mine, upper, lower, starts, send = run_first(batches, distances, field, orders)
    kept = [mine, mine]
    for step in range(1, groups):
        pairs = []
        for index in range(GROUP * rows):
            forward_from = (step - 1) * GROUP * rows + index
            adjoint_from = (groups - step) * GROUP * rows + index
            pairs.append((forward_from, forward_from + GROUP * rows))
            pairs.append((adjoint_from, adjoint_from - GROUP * rows))
        field = lax.ppermute(send, ("layer", "row"), pairs)
        *kept, send = [*run_next(step, groups, upper, lower, starts, field, kept), None][:3]
    return tuple(kept)


def solution(mesh):
    in_specs = (P("layer", "row", None), P("layer"), P("layer"), P(None, "row"), P(None, "row"))
    out_specs = (P("layer", None, "row"), P("layer", None, "row"))
    return jax.shard_map(
        on_device, mesh=mesh, in_specs=in_specs, out_specs=out_specs, check_vma=False
    )
```

profile of v0, /device:TPU:0, one launch (start us, length us, event | category | flops | bytes accessed | tf_op | source)
XLA Modules:
  0.0 49.8 jit_solution(14983222836289611725)
XLA Ops:
  1.9 0.9 %broadcast_select_fusion.field_ref.refs_4_ = f32[32,512]{1,0:T(8,128)S(1)} fusion(f32[32,512]{1,0:T(8,128)} %param.8, f32[32,512]{1,0:T(8,128)} %param.9, pred[]{:T(512)S(6)} %eq.3), kind=kLoop, calls=%fused_computation | loop fusion | flops 16384 | bytes 196609 | tf_op jit(solution)/shard_map/jit(_where)/select_n | solution.py:361
  2.8 0.0 copy-start
  2.8 1.2 %copy-done = bf16[1,512,1024]{2,1,0:T(8,128)(2,1)S(1)} copy-done((bf16[1,512,1024]{2,1,0:T(8,128)(2,1)S(1)}, bf16[1,512,1024]{2,1,0:T(8,128)(2,1)}, u32[]{:S(2)}) %copy-start) | copy-done | bytes 1048600
  4.0 0.3 fold.1.refs_0_
  4.4 3.1 %collective-permute-start.2 = (bf16[480,128]{1,0:T(8,128)(2,1)S(1)}, bf16[480,128]{1,0:T(8,128)(2,1)S(1)}, u32[]{:S(2)}, u32[]{:S(2)}) collective-permute-start(bf16[480,128]{1,0:T(8,128)(2,1)S(1)} %fold.1.refs_0_), channel_id=1, source_target_pairs={{0,8},{1,9},{2,10},{3,11},{4,12},{5,13},{6,14},{7,15},{8,0},{9,1},... | collective-permute-start | bytes 368648 | tf_op jit(solution)/shard_map/ppermute | solution.py:359
  7.4 1.5 %collective-permute-start.1 = (bf16[480,128]{1,0:T(8,128)(2,1)S(1)}, bf16[480,128]{1,0:T(8,128)(2,1)S(1)}, u32[]{:S(2)}, u32[]{:S(2)}) collective-permute-start(bf16[480,128]{1,0:T(8,128)(2,1)S(1)} %fold.1.refs_0_), channel_id=1, source_target_pairs={{0,4},{1,5},{2,6},{3,7},{4,0},{5,1},{6,2},{7,3},{8,12},{9,13},{10,... | collective-permute-start | bytes 368648 | tf_op jit(solution)/shard_map/ppermute | solution.py:359
  8.9 1.5 %collective-permute-start = (bf16[480,128]{1,0:T(8,128)(2,1)S(1)}, bf16[480,128]{1,0:T(8,128)(2,1)S(1)}, u32[]{:S(2)}, u32[]{:S(2)}) collective-permute-start(bf16[480,128]{1,0:T(8,128)(2,1)S(1)} %fold.1.refs_0_), channel_id=1, source_target_pairs={{0,1},{1,0},{2,3},{3,2},{4,5},{5,4},{6,7},{7,6},{8,9},{9,8},{10,11... | collective-permute-start | bytes 368648 | tf_op jit(solution)/shard_map/ppermute | solution.py:359
  10.5 0.0 collective-permute-start.7
  10.5 0.3 collective-permute-done.2.refs_3_
  10.8 1.7 %collective-permute-start.6 = (bf16[480,128]{1,0:T(8,128)(2,1)S(1)}, bf16[480,128]{1,0:T(8,128)(2,1)S(1)}, u32[]{:S(2)}, u32[]{:S(2)}) collective-permute-start(bf16[480,128]{1,0:T(8,128)(2,1)S(1)} %collective-permute-done.2.refs_3_), channel_id=1, source_target_pairs={{0,4},{1,5},{2,6},{3,7},{4,0},{5,1},{6,2},{7,3},{8,12},{9,13},{10,... | collective-permute-start | bytes 368648 | tf_op jit(solution)/shard_map/ppermute | solution.py:359
  12.4 0.3 collective-permute-done.1.refs_2_
  12.7 1.5 %collective-permute-start.4 = (bf16[480,128]{1,0:T(8,128)(2,1)S(1)}, bf16[480,128]{1,0:T(8,128)(2,1)S(1)}, u32[]{:S(2)}, u32[]{:S(2)}) collective-permute-start(bf16[480,128]{1,0:T(8,128)(2,1)S(1)} %collective-permute-done.1.refs_2_), channel_id=1, source_target_pairs={{0,1},{1,0},{2,3},{3,2},{4,5},{5,4},{6,7},{7,6},{8,9},{9,8},{10,11... | collective-permute-start | bytes 368648 | tf_op jit(solution)/shard_map/ppermute | solution.py:359
  14.3 1.9 %collective-permute-done.refs_1_ = bf16[480,128]{1,0:T(8,128)(2,1)S(1)} collective-permute-done((bf16[480,128]{1,0:T(8,128)(2,1)S(1)}, bf16[480,128]{1,0:T(8,128)(2,1)S(1)}, u32[]{:S(2)}, u32[]{:S(2)}) %collective-permute-start) | collective-permute-done | bytes 122912 | tf_op jit(solution)/shard_map/ppermute | solution.py:359
  16.2 0.1 collective-permute-start.3
  16.3 2.2 %collective-permute-done.7.refs_3_ = bf16[480,128]{1,0:T(8,128)(2,1)S(1)} collective-permute-done((bf16[480,128]{1,0:T(8,128)(2,1)S(1)}, bf16[480,128]{1,0:T(8,128)(2,1)S(1)}, u32[]{:S(2)}, u32[]{:S(2)}) %collective-permute-start.7) | collective-permute-done | bytes 122912 | tf_op jit(solution)/shard_map/ppermute | solution.py:359
  18.5 0.6 %collective-permute-done.4.refs_0_ = bf16[480,128]{1,0:T(8,128)(2,1)S(1)} collective-permute-done((bf16[480,128]{1,0:T(8,128)(2,1)S(1)}, bf16[480,128]{1,0:T(8,128)(2,1)S(1)}, u32[]{:S(2)}, u32[]{:S(2)}) %collective-permute-start.4) | collective-permute-done | bytes 122912 | tf_op jit(solution)/shard_map/ppermute | solution.py:359
  19.1 1.9 %collective-permute-done.5.refs_1_ = bf16[480,128]{1,0:T(8,128)(2,1)S(1)} collective-permute-done((bf16[480,128]{1,0:T(8,128)(2,1)S(1)}, bf16[480,128]{1,0:T(8,128)(2,1)S(1)}, u32[]{:S(2)}, u32[]{:S(2)}) %collective-permute-start.5) | collective-permute-done | bytes 122912 | tf_op jit(solution)/shard_map/ppermute | solution.py:359
  21.1 0.1 collective-permute-start.8
  21.1 0.0 collective-permute-done.3.refs_1_
  21.2 1.8 %collective-permute-done.8.refs_3_ = bf16[4,480,128]{2,1,0:T(8,128)(2,1)S(1)} collective-permute-done((bf16[4,480,128]{2,1,0:T(8,128)(2,1)S(1)}, bf16[4,480,128]{2,1,0:T(8,128)(2,1)S(1)}, u32[]{:S(2)}, u32[]{:S(2)}) %collective-permute-start.8) | collective-permute-done | bytes 491552 | tf_op jit(solution)/shard_map/ppermute | solution.py:359
  23.0 9.6 %cascade_first.1 = (f32[1,32,512]{2,1,0:T(8,128)S(1)}, bf16[8,8,128,256]{3,2,1,0:T(8,128)(2,1)S(1)}, bf16[8,8,128,256]{3,2,1,0:T(8,128)(2,1)S(1)}, s32[8,128]{1,0:T(8,128)S(1)}, bf16[32,1024]{1,0:T(8,128)(2,1)S(1)}) custom-call(bf16[4,480,128]{2,1,0:T(8,128)(2,1)S(1)} %batch.2.refs_0_, bf16[4,480,128]{2,1,0:T(8,128)(2,1)S(1)} %collective-permute-done.3.refs_1_, ...), custom_call_target="tpu_custom_call" | custom-call | tf_op jit(solution)/shard_map/cascade_first/pallas_call | solution.py:275
  32.6 2.7 %collective-permute-start.9 = (bf16[32,1024]{1,0:T(8,128)(2,1)S(1)}, bf16[32,1024]{1,0:T(8,128)(2,1)S(1)}, u32[]{:S(2)}, u32[]{:S(2)}) collective-permute-start(bf16[32,1024]{1,0:T(8,128)(2,1)S(1)} %get-tuple-element.10), channel_id=1, source_target_pairs={{0,16},{16,0},{1,17},{17,1},{2,18},{18,2},{3,19},{19,3},{4,20},{20... | collective-permute-start | bytes 196616 | tf_op jit(solution)/shard_map/ppermute | solution.py:374
  35.2 3.3 %collective-permute-done.9.refs_3_ = bf16[32,1024]{1,0:T(8,128)(2,1)S(1)} collective-permute-done((bf16[32,1024]{1,0:T(8,128)(2,1)S(1)}, bf16[32,1024]{1,0:T(8,128)(2,1)S(1)}, u32[]{:S(2)}, u32[]{:S(2)}) %collective-permute-start.9) | collective-permute-done | bytes 65568 | tf_op jit(solution)/shard_map/ppermute | solution.py:374
  38.5 11.3 %cascade_1.1 = (f32[1,32,512]{2,1,0:T(8,128)}, f32[1,32,512]{2,1,0:T(8,128)}) custom-call(bf16[8,8,128,256]{3,2,1,0:T(8,128)(2,1)S(1)} %get-tuple-element.7.refs_0_, bf16[8,8,128,256]{3,2,1,0:T(8,128)(2,1)S(1)} %get-tuple-element.8.refs_1_, s32[8,128]{1,0:T(8,128)S(1)} %get-tuple-element.9.refs_2_, bf16[32,1024]{1,0:T(8,128)(2,1)S(1)} %collective-permute-done.9.refs_3_, ...), custom_call_target="tpu_custom_call" | custom-call | tf_op jit(solution)/shard_map/cascade_1/pallas_call | solution.py:304
  (4 shorter events, 0.1 us)
Async XLA Ops:
  2.8 1.2 %copy-start = (bf16[1,512,1024]{2,1,0:T(8,128)(2,1)S(1)}, bf16[1,512,1024]{2,1,0:T(8,128)(2,1)}, u32[]{:S(2)}) copy-start(bf16[1,512,1024]{2,1,0:T(8,128)(2,1)} %coupling_ref.1) | copy-start | bytes 3145732
  4.4 6.4 %collective-permute-start.2 = (bf16[480,128]{1,0:T(8,128)(2,1)S(1)}, bf16[480,128]{1,0:T(8,128)(2,1)S(1)}, u32[]{:S(2)}, u32[]{:S(2)}) collective-permute-start(bf16[480,128]{1,0:T(8,128)(2,1)S(1)} %fold.1.refs_0_), channel_id=1, source_target_pairs={{0,8},{1,9},{2,10},{3,11},{4,12},{5,13},{6,14},{7,15},{8,0},{9,1},... | collective-permute-start | bytes 368648 | tf_op jit(solution)/shard_map/ppermute | solution.py:359
  7.4 5.3 %collective-permute-start.1 = (bf16[480,128]{1,0:T(8,128)(2,1)S(1)}, bf16[480,128]{1,0:T(8,128)(2,1)S(1)}, u32[]{:S(2)}, u32[]{:S(2)}) collective-permute-start(bf16[480,128]{1,0:T(8,128)(2,1)S(1)} %fold.1.refs_0_), channel_id=1, source_target_pairs={{0,4},{1,5},{2,6},{3,7},{4,0},{5,1},{6,2},{7,3},{8,12},{9,13},{10,... | collective-permute-start | bytes 368648 | tf_op jit(solution)/shard_map/ppermute | solution.py:359
  8.9 7.2 %collective-permute-start = (bf16[480,128]{1,0:T(8,128)(2,1)S(1)}, bf16[480,128]{1,0:T(8,128)(2,1)S(1)}, u32[]{:S(2)}, u32[]{:S(2)}) collective-permute-start(bf16[480,128]{1,0:T(8,128)(2,1)S(1)} %fold.1.refs_0_), channel_id=1, source_target_pairs={{0,1},{1,0},{2,3},{3,2},{4,5},{5,4},{6,7},{7,6},{8,9},{9,8},{10,11... | collective-permute-start | bytes 368648 | tf_op jit(solution)/shard_map/ppermute | solution.py:359
  10.5 8.0 %collective-permute-start.7 = (bf16[480,128]{1,0:T(8,128)(2,1)S(1)}, bf16[480,128]{1,0:T(8,128)(2,1)S(1)}, u32[]{:S(2)}, u32[]{:S(2)}) collective-permute-start(bf16[480,128]{1,0:T(8,128)(2,1)S(1)} %fold.1.refs_0_), channel_id=1, source_target_pairs={{0,13},{1,12},{2,15},{3,14},{4,9},{5,8},{6,11},{7,10},{8,5},{9,4},... | collective-permute-start | bytes 368648 | tf_op jit(solution)/shard_map/ppermute | solution.py:359
  10.8 7.7 %collective-permute-start.6 = (bf16[480,128]{1,0:T(8,128)(2,1)S(1)}, bf16[480,128]{1,0:T(8,128)(2,1)S(1)}, u32[]{:S(2)}, u32[]{:S(2)}) collective-permute-start(bf16[480,128]{1,0:T(8,128)(2,1)S(1)} %collective-permute-done.2.refs_3_), channel_id=1, source_target_pairs={{0,4},{1,5},{2,6},{3,7},{4,0},{5,1},{6,2},{7,3},{8,12},{9,13},{10,... | collective-permute-start | bytes 368648 | tf_op jit(solution)/shard_map/ppermute | solution.py:359
  12.7 6.3 %collective-permute-start.4 = (bf16[480,128]{1,0:T(8,128)(2,1)S(1)}, bf16[480,128]{1,0:T(8,128)(2,1)S(1)}, u32[]{:S(2)}, u32[]{:S(2)}) collective-permute-start(bf16[480,128]{1,0:T(8,128)(2,1)S(1)} %collective-permute-done.1.refs_2_), channel_id=1, source_target_pairs={{0,1},{1,0},{2,3},{3,2},{4,5},{5,4},{6,7},{7,6},{8,9},{9,8},{10,11... | collective-permute-start | bytes 368648 | tf_op jit(solution)/shard_map/ppermute | solution.py:359
  16.2 4.9 %collective-permute-start.5 = (bf16[480,128]{1,0:T(8,128)(2,1)S(1)}, bf16[480,128]{1,0:T(8,128)(2,1)S(1)}, u32[]{:S(2)}, u32[]{:S(2)}) collective-permute-start(bf16[480,128]{1,0:T(8,128)(2,1)S(1)} %collective-permute-done.refs_1_), channel_id=1, source_target_pairs={{0,8},{1,9},{2,10},{3,11},{4,12},{5,13},{6,14},{7,15},{8,0},{9,1},... | collective-permute-start | bytes 368648 | tf_op jit(solution)/shard_map/ppermute | solution.py:359
  16.2 5.0 %collective-permute-start.3 = (bf16[4,480,128]{2,1,0:T(8,128)(2,1)S(1)}, bf16[4,480,128]{2,1,0:T(8,128)(2,1)S(1)}, u32[]{:S(2)}, u32[]{:S(2)}) collective-permute-start(bf16[4,480,128]{2,1,0:T(8,128)(2,1)S(1)} %batch.2.refs_0_), channel_id=1, source_target_pairs={{0,2},{1,3},{2,0},{3,1},{4,6},{5,7},{6,4},{7,5},{8,10},{9,11},{10,... | collective-permute-start | bytes 1474568 | tf_op jit(solution)/shard_map/ppermute | solution.py:359
  21.1 1.9 %collective-permute-start.8 = (bf16[4,480,128]{2,1,0:T(8,128)(2,1)S(1)}, bf16[4,480,128]{2,1,0:T(8,128)(2,1)S(1)}, u32[]{:S(2)}, u32[]{:S(2)}) collective-permute-start(bf16[4,480,128]{2,1,0:T(8,128)(2,1)S(1)} %batch.3.refs_2_), channel_id=1, source_target_pairs={{0,2},{1,3},{2,0},{3,1},{4,6},{5,7},{6,4},{7,5},{8,10},{9,11},{10,... | collective-permute-start | bytes 1474568 | tf_op jit(solution)/shard_map/ppermute | solution.py:359
  32.6 5.9 %collective-permute-start.9 = (bf16[32,1024]{1,0:T(8,128)(2,1)S(1)}, bf16[32,1024]{1,0:T(8,128)(2,1)S(1)}, u32[]{:S(2)}, u32[]{:S(2)}) collective-permute-start(bf16[32,1024]{1,0:T(8,128)(2,1)S(1)} %get-tuple-element.10), channel_id=1, source_target_pairs={{0,16},{16,0},{1,17},{17,1},{2,18},{18,2},{3,19},{19,3},{4,20},{20... | collective-permute-start | bytes 196616 | tf_op jit(solution)/shard_map/ppermute | solution.py:374
where the time goes:
time: 50 us; the launch traced here: 49.8 us
  Pallas kernels  21.2 us (42%)
  waiting for transfers between devices  12.4 us (25%)
  starting transfers between devices  12.1 us (24%)
  between operations  2 us (4%)
  local copies, waits for them, and re-layouts  1.22 us (2%)
  other arithmetic  0.86 us (2%)
    pallas_call x1, Pallas kernels, run_next(): pl.pallas_call(functools.partial(cascade_next_kernel, step, groups), out_...  11.3 us
    pallas_call x1, Pallas kernels, run_first(): pl.pallas_call(functools.partial(cascade_first_kernel, distances), out_sh...  9.57 us
    ppermute x9, starting transfers between devices, across(): return lax.ppermute(array, ('layer', 'row'), pairs)  9.4 us
    ppermute x9, waiting for transfers between devices, across(): return lax.ppermute(array, ('layer', 'row'), pairs)  9.12 us
    ppermute x1, waiting for transfers between devices, on_device(): field = lax.ppermute(send, ('layer', 'row'), pairs)  3.28 us
    ppermute x1, starting transfers between devices, on_device(): field = lax.ppermute(send, ('layer', 'row'), pairs)  2.66 us
    unnamed x2, local copies, waits for them, and re-layouts  1.22 us
  transfers between devices with their start and end apart: 10, of which 8 were waited for; matrix products, arithmetic and copies ran while one was open for 0% of the time, Pallas kernels for 0%

commit v1 on v0

--- a/solution.py
+++ b/solution.py
@@ -219,7 +219,7 @@
     def prepare(k):
         slot = jnp.where(forward, k, GROUP - 1 - k)
         start = expand(folds, slot, masks, upper.at[k], lower.at[k])
-        starts[k : k + 1, :] = jnp.full((1, LANES), start, jnp.int32)
+        starts[k] = start
         return start
 
     start = prepare(0)
@@ -241,12 +241,9 @@
     x = field[...].astype(jnp.float32)
     x = [x[:, u : u + LANES] for u in range(0, x.shape[1], LANES)]
 
-    def layer(k, x):
+    for k in range(GROUP):
         at = jnp.where(same_order, k, GROUP - 1 - k)
-        start = jnp.max(starts[pl.ds(at, 1), :])
-        return run_layer(x, sign, upper.at[at], lower.at[at], start, xs, zs)
-
-    x = lax.fori_loop(0, GROUP, layer, x)
+        x = run_layer(x, sign, upper.at[at], lower.at[at], starts[at], xs, zs)
     finish(x, new_forward, *send)
     mine = new_forward[0]
     new_forward[0] = jnp.where(forward, mine, kept_forward[0])
@@ -278,11 +275,11 @@
             jax.ShapeDtypeStruct((1, count, panel), jnp.float32),
             window,
             window,
-            jax.ShapeDtypeStruct((GROUP, LANES), jnp.int32),
+            jax.ShapeDtypeStruct((GROUP,), jnp.int32),
             jax.ShapeDtypeStruct((count, orders), jnp.bfloat16),
         ],
         in_specs=[vmem] * (len(batches) + 1),
-        out_specs=[vmem] * 5,
+        out_specs=[vmem, vmem, vmem, pl.BlockSpec(memory_space=pltpu.SMEM), vmem],
         scratch_shapes=[
             pltpu.VMEM((GROUP, tiles * PACKED, LANES), jnp.bfloat16),
             pltpu.VMEM((4, LANES, LANES), jnp.bfloat16),
@@ -304,7 +301,7 @@
     return pl.pallas_call(
         functools.partial(cascade_next_kernel, step, groups),
         out_shape=out_shape,
-        in_specs=[vmem] * 6,
+        in_specs=[vmem, vmem, pl.BlockSpec(memory_space=pltpu.SMEM), vmem, vmem, vmem],
         out_specs=[vmem] * len(out_shape),
         scratch_shapes=[
             pltpu.VMEM((tiles, count, LANES), jnp.bfloat16),
@@ -326,16 +323,15 @@
     def distance(subset):
         return tuple(sum(bits[b][axis] for b in members(subset)) for axis in (0, 1))
 
-    subsets = sorted(range(1 << count), key=lambda m: (m.bit_count(), m))
     pieces = {0: own}
-    for subset in subsets[1 : count + 1] + subsets[-1:]:
-        pieces[subset] = across(own, *distance(subset))
-    for subset in subsets[count + 1 : -1]:
-        which = members(subset)
-        link = next((b for b in which if (b + 1) % count in which), which[0])
-        pieces[subset] = across(pieces[subset ^ 1 << link], *distance(1 << link))
     batches, counts, distances = [], [], []
-    for part in (subsets[: count + 1], subsets[count + 1 :]):
+    for number in range(1, count + 1):
+        part = [m for m in range(1 << count) if m.bit_count() == number]
+        for subset in part:
+            which = members(subset)
+            link = next((b for b in which if (b + 1) % count in which), which[0])
+            pieces[subset] = across(pieces[subset ^ 1 << link], *distance(1 << link))
+        part = [0] + part if number == 1 else part
         mine = batch([pieces[subset] for subset in part])
         batches += [mine, across(mine, 1, 0)]
         counts += [len(part), len(part)]

time: 50 us -> 53.3 us (1.066)
  starting transfers between devices: 12.1 us -> 15.2 us
  waiting for transfers between devices: 12.4 us -> 13 us
    ppermute x9 -> x10, starting transfers between devices: 9.4 us -> 12.6 us  [across(): return lax.ppermute(array, ('layer', 'row'), pairs)]
    pallas_call x1, Pallas kernels: 11.3 us -> 10.4 us  [run_next(): pl.pallas_call(functools.partial(cascade_next_kernel, step, groups), out_...]
    ppermute x1, waiting for transfers between devices: 3.28 us -> 3.97 us  [on_device(): field = lax.ppermute(send, ('layer', 'row'), pairs)]
    ppermute x9 -> x10, waiting for transfers between devices: 9.12 us -> 9.03 us  [across(): return lax.ppermute(array, ('layer', 'row'), pairs)]
  transfers between devices with their start and end apart: 10 -> 11, of which waited for: 8 -> 6; matrix products, arithmetic and copies ran while one was open for 0% -> 0% of each run, Pallas kernels for 0% -> 0%
where the time goes in v1:
time: 53.3 us; the launch traced here: 53.1 us
  Pallas kernels  20.8 us (39%)
  starting transfers between devices  15.2 us (29%)
  waiting for transfers between devices  13 us (24%)
  between operations  2.01 us (4%)
  local copies, waits for them, and re-layouts  1.22 us (2%)
  other arithmetic  0.86 us (2%)
    ppermute x10, starting transfers between devices, across(): return lax.ppermute(array, ('layer', 'row'), pairs)  12.6 us
    pallas_call x1, Pallas kernels, run_next(): pl.pallas_call(functools.partial(cascade_next_kernel, step, groups), out_...  10.4 us
    pallas_call x1, Pallas kernels, run_first(): pl.pallas_call(functools.partial(cascade_first_kernel, distances), out_sh...  10 us
    ppermute x10, waiting for transfers between devices, across(): return lax.ppermute(array, ('layer', 'row'), pairs)  9.03 us
    ppermute x1, waiting for transfers between devices, on_device(): field = lax.ppermute(send, ('layer', 'row'), pairs)  3.97 us
    ppermute x1, starting transfers between devices, on_device(): field = lax.ppermute(send, ('layer', 'row'), pairs)  2.67 us
    unnamed x2, local copies, waits for them, and re-layouts  1.22 us
  transfers between devices with their start and end apart: 11, of which 6 were waited for; matrix products, arithmetic and copies ran while one was open for 0% of the time, Pallas kernels for 0%

profile of v1, /device:TPU:0, one launch (start us, length us, event | category | flops | bytes accessed | tf_op | source)
XLA Modules:
  0.0 53.1 jit_solution(11241095862308769411)
XLA Ops:
  1.9 0.9 %broadcast_select_fusion.field_ref.refs_6_ = f32[32,512]{1,0:T(8,128)S(1)} fusion(f32[32,512]{1,0:T(8,128)} %param.8, f32[32,512]{1,0:T(8,128)} %param.9, pred[]{:T(512)S(6)} %eq.3), kind=kLoop, calls=%fused_computation | loop fusion | flops 16384 | bytes 196609 | tf_op jit(solution)/shard_map/jit(_where)/select_n | solution.py:357
  2.8 0.0 copy-start
  2.8 1.2 %copy-done = bf16[1,512,1024]{2,1,0:T(8,128)(2,1)S(1)} copy-done((bf16[1,512,1024]{2,1,0:T(8,128)(2,1)S(1)}, bf16[1,512,1024]{2,1,0:T(8,128)(2,1)}, u32[]{:S(2)}) %copy-start) | copy-done | bytes 1048600
  4.0 0.3 fold.1.refs_0_
  4.4 3.1 %collective-permute-start.2 = (bf16[480,128]{1,0:T(8,128)(2,1)S(1)}, bf16[480,128]{1,0:T(8,128)(2,1)S(1)}, u32[]{:S(2)}, u32[]{:S(2)}) collective-permute-start(bf16[480,128]{1,0:T(8,128)(2,1)S(1)} %fold.1.refs_0_), channel_id=1, source_target_pairs={{0,8},{1,9},{2,10},{3,11},{4,12},{5,13},{6,14},{7,15},{8,0},{9,1},... | collective-permute-start | bytes 368648 | tf_op jit(solution)/shard_map/ppermute | solution.py:355
  7.4 1.5 %collective-permute-start.1 = (bf16[480,128]{1,0:T(8,128)(2,1)S(1)}, bf16[480,128]{1,0:T(8,128)(2,1)S(1)}, u32[]{:S(2)}, u32[]{:S(2)}) collective-permute-start(bf16[480,128]{1,0:T(8,128)(2,1)S(1)} %fold.1.refs_0_), channel_id=1, source_target_pairs={{0,4},{1,5},{2,6},{3,7},{4,0},{5,1},{6,2},{7,3},{8,12},{9,13},{10,... | collective-permute-start | bytes 368648 | tf_op jit(solution)/shard_map/ppermute | solution.py:355
  8.9 1.5 %collective-permute-start = (bf16[480,128]{1,0:T(8,128)(2,1)S(1)}, bf16[480,128]{1,0:T(8,128)(2,1)S(1)}, u32[]{:S(2)}, u32[]{:S(2)}) collective-permute-start(bf16[480,128]{1,0:T(8,128)(2,1)S(1)} %fold.1.refs_0_), channel_id=1, source_target_pairs={{0,1},{1,0},{2,3},{3,2},{4,5},{5,4},{6,7},{7,6},{8,9},{9,8},{10,11... | collective-permute-start | bytes 368648 | tf_op jit(solution)/shard_map/ppermute | solution.py:355
  10.5 0.3 collective-permute-done.2.refs_3_
  10.8 1.7 %collective-permute-start.6 = (bf16[480,128]{1,0:T(8,128)(2,1)S(1)}, bf16[480,128]{1,0:T(8,128)(2,1)S(1)}, u32[]{:S(2)}, u32[]{:S(2)}) collective-permute-start(bf16[480,128]{1,0:T(8,128)(2,1)S(1)} %collective-permute-done.2.refs_3_), channel_id=1, source_target_pairs={{0,4},{1,5},{2,6},{3,7},{4,0},{5,1},{6,2},{7,3},{8,12},{9,13},{10,... | collective-permute-start | bytes 368648 | tf_op jit(solution)/shard_map/ppermute | solution.py:355
  12.4 1.5 %collective-permute-start.4 = (bf16[480,128]{1,0:T(8,128)(2,1)S(1)}, bf16[480,128]{1,0:T(8,128)(2,1)S(1)}, u32[]{:S(2)}, u32[]{:S(2)}) collective-permute-start(bf16[480,128]{1,0:T(8,128)(2,1)S(1)} %collective-permute-done.1.refs_2_), channel_id=1, source_target_pairs={{0,1},{1,0},{2,3},{3,2},{4,5},{5,4},{6,7},{7,6},{8,9},{9,8},{10,11... | collective-permute-start | bytes 368648 | tf_op jit(solution)/shard_map/ppermute | solution.py:355
  13.9 1.6 %collective-permute-start.5 = (bf16[480,128]{1,0:T(8,128)(2,1)S(1)}, bf16[480,128]{1,0:T(8,128)(2,1)S(1)}, u32[]{:S(2)}, u32[]{:S(2)}) collective-permute-start(bf16[480,128]{1,0:T(8,128)(2,1)S(1)} %collective-permute-done.refs_1_), channel_id=1, source_target_pairs={{0,8},{1,9},{2,10},{3,11},{4,12},{5,13},{6,14},{7,15},{8,0},{9,1},... | collective-permute-start | bytes 368648 | tf_op jit(solution)/shard_map/ppermute | solution.py:355
  15.6 0.1 collective-permute-start.3
  15.6 0.0 collective-permute-done.6.refs_2_
  15.6 1.7 %collective-permute-done.4.refs_0_ = bf16[480,128]{1,0:T(8,128)(2,1)S(1)} collective-permute-done((bf16[480,128]{1,0:T(8,128)(2,1)S(1)}, bf16[480,128]{1,0:T(8,128)(2,1)S(1)}, u32[]{:S(2)}, u32[]{:S(2)}) %collective-permute-start.4) | collective-permute-done | bytes 122912 | tf_op jit(solution)/shard_map/ppermute | solution.py:355
  17.3 1.5 %collective-permute-done.5.refs_1_ = bf16[480,128]{1,0:T(8,128)(2,1)S(1)} collective-permute-done((bf16[480,128]{1,0:T(8,128)(2,1)S(1)}, bf16[480,128]{1,0:T(8,128)(2,1)S(1)}, u32[]{:S(2)}, u32[]{:S(2)}) %collective-permute-start.5) | collective-permute-done | bytes 122912 | tf_op jit(solution)/shard_map/ppermute | solution.py:355
  18.9 0.1 collective-permute-start.7
  18.9 1.5 %collective-permute-start.8 = (bf16[480,128]{1,0:T(8,128)(2,1)S(1)}, bf16[480,128]{1,0:T(8,128)(2,1)S(1)}, u32[]{:S(2)}, u32[]{:S(2)}) collective-permute-start(bf16[480,128]{1,0:T(8,128)(2,1)S(1)} %collective-permute-done.6.refs_2_), channel_id=1, source_target_pairs={{0,1},{1,0},{2,3},{3,2},{4,5},{5,4},{6,7},{7,6},{8,9},{9,8},{10,11... | collective-permute-start | bytes 368648 | tf_op jit(solution)/shard_map/ppermute | solution.py:355
  20.5 4.2 %collective-permute-done.8.refs_0_ = bf16[480,128]{1,0:T(8,128)(2,1)S(1)} collective-permute-done((bf16[480,128]{1,0:T(8,128)(2,1)S(1)}, bf16[480,128]{1,0:T(8,128)(2,1)S(1)}, u32[]{:S(2)}, u32[]{:S(2)}) %collective-permute-start.8) | collective-permute-done | bytes 122912 | tf_op jit(solution)/shard_map/ppermute | solution.py:355
  24.7 0.1 collective-permute-start.9
  24.8 1.3 %collective-permute-done.9.refs_5_ = bf16[1,480,128]{2,1,0:T(8,128)(2,1)S(1)} collective-permute-done((bf16[1,480,128]{2,1,0:T(8,128)(2,1)S(1)}, bf16[1,480,128]{2,1,0:T(8,128)(2,1)S(1)}, u32[]{:S(2)}, u32[]{:S(2)}) %collective-permute-start.9) | collective-permute-done | bytes 122912 | tf_op jit(solution)/shard_map/ppermute | solution.py:355
  26.1 10.0 %cascade_first.1 = (f32[1,32,512]{2,1,0:T(8,128)S(1)}, bf16[8,8,128,256]{3,2,1,0:T(8,128)(2,1)S(1)}, bf16[8,8,128,256]{3,2,1,0:T(8,128)(2,1)S(1)}, s32[8]{0:T(128)S(1)}, bf16[32,1024]{1,0:T(8,128)(2,1)S(1)}) custom-call(bf16[4,480,128]{2,1,0:T(8,128)(2,1)S(1)} %batch.3.refs_0_, bf16[4,480,128]{2,1,0:T(8,128)(2,1)S(1)} %collective-permute-done.3.refs_1_, ...), custom_call_target="tpu_custom_call" | custom-call | tf_op jit(solution)/shard_map/cascade_first/pallas_call | solution.py:272
  36.1 2.7 %collective-permute-start.10 = (bf16[32,1024]{1,0:T(8,128)(2,1)S(1)}, bf16[32,1024]{1,0:T(8,128)(2,1)S(1)}, u32[]{:S(2)}, u32[]{:S(2)}) collective-permute-start(bf16[32,1024]{1,0:T(8,128)(2,1)S(1)} %get-tuple-element.10), channel_id=1, source_target_pairs={{0,16},{16,0},{1,17},{17,1},{2,18},{18,2},{3,19},{19,3},{4,20},{20... | collective-permute-start | bytes 196616 | tf_op jit(solution)/shard_map/ppermute | solution.py:370
  38.8 4.0 %collective-permute-done.10.refs_3_ = bf16[32,1024]{1,0:T(8,128)(2,1)S(1)} collective-permute-done((bf16[32,1024]{1,0:T(8,128)(2,1)S(1)}, bf16[32,1024]{1,0:T(8,128)(2,1)S(1)}, u32[]{:S(2)}, u32[]{:S(2)}) %collective-permute-start.10) | collective-permute-done | bytes 65568 | tf_op jit(solution)/shard_map/ppermute | solution.py:370
  42.8 10.4 %cascade_1.1 = (f32[1,32,512]{2,1,0:T(8,128)}, f32[1,32,512]{2,1,0:T(8,128)}) custom-call(bf16[8,8,128,256]{3,2,1,0:T(8,128)(2,1)S(1)} %get-tuple-element.7.refs_0_, bf16[8,8,128,256]{3,2,1,0:T(8,128)(2,1)S(1)} %get-tuple-element.8.refs_1_, s32[8]{0:T(128)S(1)} %get-tuple-element.9.refs_2_, bf16[32,1024]{1,0:T(8,128)(2,1)S(1)} %collective-permute-done.10.refs_3_, ...), custom_call_target="tpu_custom_call" | custom-call | tf_op jit(solution)/shard_map/cascade_1/pallas_call | solution.py:301
  (7 shorter events, 0.1 us)
Async XLA Ops:
  2.8 1.2 %copy-start = (bf16[1,512,1024]{2,1,0:T(8,128)(2,1)S(1)}, bf16[1,512,1024]{2,1,0:T(8,128)(2,1)}, u32[]{:S(2)}) copy-start(bf16[1,512,1024]{2,1,0:T(8,128)(2,1)} %coupling_ref.1) | copy-start | bytes 3145732
  4.4 6.4 %collective-permute-start.2 = (bf16[480,128]{1,0:T(8,128)(2,1)S(1)}, bf16[480,128]{1,0:T(8,128)(2,1)S(1)}, u32[]{:S(2)}, u32[]{:S(2)}) collective-permute-start(bf16[480,128]{1,0:T(8,128)(2,1)S(1)} %fold.1.refs_0_), channel_id=1, source_target_pairs={{0,8},{1,9},{2,10},{3,11},{4,12},{5,13},{6,14},{7,15},{8,0},{9,1},... | collective-permute-start | bytes 368648 | tf_op jit(solution)/shard_map/ppermute | solution.py:355
  7.4 5.0 %collective-permute-start.1 = (bf16[480,128]{1,0:T(8,128)(2,1)S(1)}, bf16[480,128]{1,0:T(8,128)(2,1)S(1)}, u32[]{:S(2)}, u32[]{:S(2)}) collective-permute-start(bf16[480,128]{1,0:T(8,128)(2,1)S(1)} %fold.1.refs_0_), channel_id=1, source_target_pairs={{0,4},{1,5},{2,6},{3,7},{4,0},{5,1},{6,2},{7,3},{8,12},{9,13},{10,... | collective-permute-start | bytes 368648 | tf_op jit(solution)/shard_map/ppermute | solution.py:355
  8.9 5.0 %collective-permute-start = (bf16[480,128]{1,0:T(8,128)(2,1)S(1)}, bf16[480,128]{1,0:T(8,128)(2,1)S(1)}, u32[]{:S(2)}, u32[]{:S(2)}) collective-permute-start(bf16[480,128]{1,0:T(8,128)(2,1)S(1)} %fold.1.refs_0_), channel_id=1, source_target_pairs={{0,1},{1,0},{2,3},{3,2},{4,5},{5,4},{6,7},{7,6},{8,9},{9,8},{10,11... | collective-permute-start | bytes 368648 | tf_op jit(solution)/shard_map/ppermute | solution.py:355
  10.8 4.9 %collective-permute-start.6 = (bf16[480,128]{1,0:T(8,128)(2,1)S(1)}, bf16[480,128]{1,0:T(8,128)(2,1)S(1)}, u32[]{:S(2)}, u32[]{:S(2)}) collective-permute-start(bf16[480,128]{1,0:T(8,128)(2,1)S(1)} %collective-permute-done.2.refs_3_), channel_id=1, source_target_pairs={{0,4},{1,5},{2,6},{3,7},{4,0},{5,1},{6,2},{7,3},{8,12},{9,13},{10,... | collective-permute-start | bytes 368648 | tf_op jit(solution)/shard_map/ppermute | solution.py:355
  12.4 4.9 %collective-permute-start.4 = (bf16[480,128]{1,0:T(8,128)(2,1)S(1)}, bf16[480,128]{1,0:T(8,128)(2,1)S(1)}, u32[]{:S(2)}, u32[]{:S(2)}) collective-permute-start(bf16[480,128]{1,0:T(8,128)(2,1)S(1)} %collective-permute-done.1.refs_2_), channel_id=1, source_target_pairs={{0,1},{1,0},{2,3},{3,2},{4,5},{5,4},{6,7},{7,6},{8,9},{9,8},{10,11... | collective-permute-start | bytes 368648 | tf_op jit(solution)/shard_map/ppermute | solution.py:355
  13.9 4.9 %collective-permute-start.5 = (bf16[480,128]{1,0:T(8,128)(2,1)S(1)}, bf16[480,128]{1,0:T(8,128)(2,1)S(1)}, u32[]{:S(2)}, u32[]{:S(2)}) collective-permute-start(bf16[480,128]{1,0:T(8,128)(2,1)S(1)} %collective-permute-done.refs_1_), channel_id=1, source_target_pairs={{0,8},{1,9},{2,10},{3,11},{4,12},{5,13},{6,14},{7,15},{8,0},{9,1},... | collective-permute-start | bytes 368648 | tf_op jit(solution)/shard_map/ppermute | solution.py:355
  15.6 10.5 %collective-permute-start.3 = (bf16[4,480,128]{2,1,0:T(8,128)(2,1)S(1)}, bf16[4,480,128]{2,1,0:T(8,128)(2,1)S(1)}, u32[]{:S(2)}, u32[]{:S(2)}) collective-permute-start(bf16[4,480,128]{2,1,0:T(8,128)(2,1)S(1)} %batch.3.refs_0_), channel_id=1, source_target_pairs={{0,2},{1,3},{2,0},{3,1},{4,6},{5,7},{6,4},{7,5},{8,10},{9,11},{10,... | collective-permute-start | bytes 1474568 | tf_op jit(solution)/shard_map/ppermute | solution.py:355
  18.9 7.2 %collective-permute-start.7 = (bf16[3,480,128]{2,1,0:T(8,128)(2,1)S(1)}, bf16[3,480,128]{2,1,0:T(8,128)(2,1)S(1)}, u32[]{:S(2)}, u32[]{:S(2)}) collective-permute-start(bf16[3,480,128]{2,1,0:T(8,128)(2,1)S(1)} %batch.4.refs_2_), channel_id=1, source_target_pairs={{0,2},{1,3},{2,0},{3,1},{4,6},{5,7},{6,4},{7,5},{8,10},{9,11},{10,... | collective-permute-start | bytes 1105928 | tf_op jit(solution)/shard_map/ppermute | solution.py:355
  18.9 5.7 %collective-permute-start.8 = (bf16[480,128]{1,0:T(8,128)(2,1)S(1)}, bf16[480,128]{1,0:T(8,128)(2,1)S(1)}, u32[]{:S(2)}, u32[]{:S(2)}) collective-permute-start(bf16[480,128]{1,0:T(8,128)(2,1)S(1)} %collective-permute-done.6.refs_2_), channel_id=1, source_target_pairs={{0,1},{1,0},{2,3},{3,2},{4,5},{5,4},{6,7},{7,6},{8,9},{9,8},{10,11... | collective-permute-start | bytes 368648 | tf_op jit(solution)/shard_map/ppermute | solution.py:355
  24.7 1.4 %collective-permute-start.9 = (bf16[1,480,128]{2,1,0:T(8,128)(2,1)S(1)}, bf16[1,480,128]{2,1,0:T(8,128)(2,1)S(1)}, u32[]{:S(2)}, u32[]{:S(2)}) collective-permute-start(bf16[1,480,128]{2,1,0:T(8,128)(2,1)S(1)} %batch.5.refs_4_), channel_id=1, source_target_pairs={{0,2},{1,3},{2,0},{3,1},{4,6},{5,7},{6,4},{7,5},{8,10},{9,11},{10,... | collective-permute-start | bytes 368648 | tf_op jit(solution)/shard_map/ppermute | solution.py:355
  36.1 6.6 %collective-permute-start.10 = (bf16[32,1024]{1,0:T(8,128)(2,1)S(1)}, bf16[32,1024]{1,0:T(8,128)(2,1)S(1)}, u32[]{:S(2)}, u32[]{:S(2)}) collective-permute-start(bf16[32,1024]{1,0:T(8,128)(2,1)S(1)} %get-tuple-element.10), channel_id=1, source_target_pairs={{0,16},{16,0},{1,17},{17,1},{2,18},{18,2},{3,19},{19,3},{4,20},{20... | collective-permute-start | bytes 196616 | tf_op jit(solution)/shard_map/ppermute | solution.py:370
